TPU v7x, 32 devices: a whole 2x2x4 slice. The times are simulated.
32 devices in a mesh: row: 4 (over z), col: 8 (over y, x, core).
Axes of the slice: x: 2, y: 2, z: 4, core: 2. Of those that a mesh axis runs over, the one named last changes fastest.
Arguments:
- trailing: bfloat16 [4096, 4096], P('row', 'col'), may hold values from -12 to 12
- panel_left: bfloat16 [4096, 1024], P(('row', 'col')), may hold values from -1.5 to 1.5
- panel_right: bfloat16 [4096, 1024], P(('col', 'row')), may hold values from -1.5 to 1.5
- inverse_factors: float32 [2, 512, 512], replicated, may hold values from -2 to 2, as said below
- active: int32 [8, 8], P('row', 'col'), may hold values 0 or 1
Outputs:
- updated: bfloat16 [4096, 4096], P('row', 'col')
Inputs may be any that keep to these rules, and one draw needn't show every extreme that they name: `inverse_factors`: lower triangular, positive diagonal.
All inputs are finite; a program needn't handle non-finite values. No bound on the sum of `active` on one device may be relied on, other than what follows from the above.
Results may differ from a plain program's by a relative error of at most 0.0052.
Values may be sent and summed in bfloat16 or wider, within the bound.
A program may use at most 64 MiB of HBM per device.

v0:
```python
import jax
import jax.numpy as jnp
from jax import lax
from jax.sharding import PartitionSpec as P


def triangle(rows, inverse_factors):
    width = inverse_factors.shape[1]
    parts = []
    for panel in range(inverse_factors.shape[0]):
        block = rows[:, panel * width : (panel + 1) * width].astype(jnp.float32)
        parts.append(
            jnp.dot(
                block,
                inverse_factors[panel].T,
                precision=lax.Precision.HIGHEST,
                preferred_element_type=jnp.float32,
            )
        )
    return jnp.concatenate(parts, axis=1).astype(jnp.bfloat16)


def outer_rows(piece, gathered):
    return lax.dot_general(
        piece, gathered, (((1,), (1,)), ((), ())), preferred_element_type=jnp.float32
    )


def local(trailing, panel_left, panel_right, inverse_factors, active):
    width = inverse_factors.shape[1]
    factor_left = triangle(panel_left, inverse_factors)
    factor_right = triangle(panel_right, inverse_factors)
    change = jnp.zeros(trailing.shape, jnp.float32)
    for panel in range(inverse_factors.shape[0]):
        right_part = lax.all_gather(
            factor_right[:, panel * width : (panel + 1) * width], "row", axis=0, tiled=True
        )
        change = change + outer_rows(
            lax.all_gather(
                factor_left[:, panel * width : (panel + 1) * width], "col", axis=0, tiled=True
            ),
            right_part,
        )
    tile_rows = active.shape[0]
    tile_cols = active.shape[1]
    shaped = trailing.astype(jnp.float32).reshape(tile_rows, width, tile_cols, width)
    fresh = shaped - change.reshape(tile_rows, width, tile_cols, width)
    keep = active[:, None, :, None] == 1
    result = jnp.where(keep, fresh, shaped).astype(jnp.bfloat16)
    return result.reshape(trailing.shape)


def solution(mesh):
    in_specs = (
        P("row", "col"),
        P(("row", "col"), None),
        P(("col", "row"), None),
        P(),
        P("row", "col"),
    )
    out_specs = P("row", "col")
    return jax.shard_map(local, mesh=mesh, in_specs=in_specs, out_specs=out_specs, check_vma=False)
```

profile of v0, /device:TPU:0, one launch (start us, length us, event | category | flops | bytes accessed | tf_op | source)
XLA Modules:
  0.0 71.3 jit_solution(9194186326282365686)
XLA Ops:
  6.5 0.0 copy-start
  6.5 0.0 copy-start.2
  6.5 0.0 copy-start.1
  6.5 0.0 all-gather.3.cloned.1.call-start
  6.5 2.8 %convolution_convert_fusion.3 = bf16[128,512]{1,0:T(8,128)(2,1)} fusion(f32[2,512,512]{2,1,0:T(8,128)} %param.8, bf16[128,1024]{1,0:T(8,128)(2,1)} %param.6), kind=kOutput, calls=%fused_computation.5 | convolution fusion | flops 402718720 | bytes 1310720 | tf_op jit(solution)/shard_map/dot_general | solution.py:13
  9.3 0.0 all-gather.3.cloned.1.call-update
  9.4 0.0 all-gather.5.cloned.1.call-start
  9.4 2.7 %convolution_convert_fusion.1 = bf16[128,512]{1,0:T(8,128)(2,1)} fusion(f32[2,512,512]{2,1,0:T(8,128)} %param.8, bf16[128,1024]{1,0:T(8,128)(2,1)} %param.6), kind=kOutput, calls=%fused_computation.3 | convolution fusion | flops 402718720 | bytes 1310720 | tf_op jit(solution)/shard_map/dot_general | solution.py:13
  12.1 0.0 all-gather.5.cloned.1.call-update
  12.1 0.0 copy-done.2
  12.1 0.1 broadcast_in_dim.13
  12.2 0.0 copy-done
  12.2 0.0 copy-done.1
  12.2 0.7 convolution_convert_fusion.2
  12.9 17.4 %all_gather.13 = bf16[512,512]{1,0:T(8,128)(2,1)S(1)} all-gather(bf16[128,512]{1,0:T(8,128)(2,1)S(1)} %convolution_convert_fusion.2), channel_id=1, replica_groups=mesh['row'=4,'col'=8] {'row'}, dimensions={0}, use_global_device_ids=true | all-gather | bytes 655360 | tf_op jit(solution)/shard_map/all_gather | solution.py:35
  30.3 0.7 convolution_convert_fusion
  31.0 16.2 %all_gather.15 = bf16[512,512]{1,0:T(8,128)(2,1)S(1)} all-gather(bf16[128,512]{1,0:T(8,128)(2,1)S(1)} %convolution_convert_fusion), channel_id=1, replica_groups=mesh['row'=4,'col'=8] {'row'}, dimensions={0}, use_global_device_ids=true | all-gather | bytes 655360 | tf_op jit(solution)/shard_map/all_gather | solution.py:35
  47.2 0.0 all-gather.3.cloned.1.call-done
  47.2 2.0 %fusion.13 = f32[1024,512]{1,0:T(8,128)S(1)} fusion(bf16[1024,512]{1,0:T(8,128)(2,1)} %all-gather.3.cloned.1.call-done, bf16[512,512]{1,0:T(8,128)(2,1)S(1)} %all_gather.13), kind=kOutput, calls=%fused_computation.19 | convolution fusion | flops 536870912 | bytes 3670016 | tf_op jit(solution)/shard_map/dot_general | solution.py:24
  49.1 12.0 %all-gather.5.cloned.1.call-done = bf16[1024,512]{1,0:T(8,128)(2,1)} async-done(((bf16[128,512]{1,0:T(8,128)(2,1)}), bf16[1024,512]{1,0:T(8,128)(2,1)}) %all-gather.5.cloned.1.call-update) | async-done | bytes 1048592 | tf_op jit(solution)/shard_map/all_gather | solution.py:39
  61.1 3.3 %fusion = bf16[1024,512]{1,0:T(8,128)(2,1)} fusion(f32[1024,512]{1,0:T(8,128)S(1)} %fusion.13, bf16[1024,512]{1,0:T(8,128)(2,1)} %param.5, bf16[1024,512]{1,0:T(8,128)(2,1)} %all-gather.5.cloned.1.call-done, bf16[512,512]{1,0:T(8,128)(2,1)S(1)} %all_gather.15, pred[1024]{0:T(1024)(128)(4,1)S(1)} %broadcast_in_dim.14), kind=kOutput, calls=%fused_computation.1 | convolution fusion | flops 539492352 | bytes 5768192 | tf_op jit(solution)/shard_map/dot_general | solution.py:24
  (2 shorter events, 0.0 us)
Async XLA Ops:
  6.5 5.7 %copy-start = (f32[2,512,512]{2,1,0:T(8,128)S(1)}, f32[2,512,512]{2,1,0:T(8,128)}, u32[]{:S(2)}) copy-start(f32[2,512,512]{2,1,0:T(8,128)} %param.8) | copy-start | bytes 6291460
  6.5 5.6 %copy-start.2 = (s32[2,1]{0,1:T(1,128)S(1)}, s32[2,1]{0,1:T(1,128)}, u32[]{:S(2)}) copy-start(s32[2,1]{0,1:T(1,128)} %param.9) | copy-start | bytes 28
  6.5 5.7 %copy-start.1 = (bf16[128,1024]{1,0:T(8,128)(2,1)S(1)}, bf16[128,1024]{1,0:T(8,128)(2,1)}, u32[]{:S(2)}) copy-start(bf16[128,1024]{1,0:T(8,128)(2,1)} %param.7) | copy-start | bytes 786436
  6.5 40.6 %all-gather.3.cloned.1.call-start = ((), (), s32[]{:S(2)}) async-start(), calls=%async_computation | async-start | bytes 1179648 | tf_op jit(solution)/shard_map/all_gather | solution.py:39
  9.4 51.8 %all-gather.5.cloned.1.call-start = ((), (), s32[]{:S(2)}) async-start(), calls=%async_computation.1 | async-start | bytes 1179648 | tf_op jit(solution)/shard_map/all_gather | solution.py:39
Sparse Core Ops, SparseCore 0:
  9.5 26.1 all-gather.2
  37.6 23.4 all-gather.4
where the time goes:
time: 71.5 us; the launch traced here: 71.3 us
  blocking collectives  33.5 us (47%)
  between operations  13.4 us (19%)
  matrix products  12.2 us (17%)
  waiting for transfers between devices  12 us (17%)
    all_gather x2, blocking collectives, local(): lax.all_gather(factor_right[:, panel * width:(panel + 1) * width], 'row',...  33.5 us
    all_gather x2, waiting for transfers between devices, local(): lax.all_gather(factor_left[:, panel * width:(panel + 1) * width], 'col',...  12 us
    dot_general x4, matrix products, triangle(): jnp.dot(block, inverse_factors[panel].T, precision=lax.Precision.HIGHEST,...  6.86 us
    dot_general x2, matrix products, outer_rows(): lax.dot_general(piece, gathered, (((1,), (1,)), ((), ())), preferred_elem...  5.3 us
  transfers between devices with their start and end apart: 2, of which 1 were waited for; matrix products, arithmetic and copies ran while one was open for 9% of the time, Pallas kernels for 0%

commit v1 on v0

v1 whole, which is shorter than its diff:
```python
import functools

import jax
import jax.numpy as jnp
from jax import lax
from jax.experimental import pallas as pl
from jax.experimental.pallas import tpu as pltpu
from jax.sharding import PartitionSpec as P

MESH = pl.DeviceIdType.MESH
NT_DIMS = (((1,), (1,)), ((), ()))


def dot_nt(a, b):
    return lax.dot_general(a, b, NT_DIMS, preferred_element_type=jnp.float32)


def triangle(rows, inverse_factors):
    width = inverse_factors.shape[1]
    parts = []
    for panel in range(inverse_factors.shape[0]):
        block = rows[:, panel * width : (panel + 1) * width].astype(jnp.float32)
        parts.append(
            jnp.dot(
                block,
                inverse_factors[panel].T,
                precision=lax.Precision.HIGHEST,
                preferred_element_type=jnp.float32,
            )
        )
    return jnp.concatenate(parts, axis=1).astype(jnp.bfloat16)


def local_plain(trailing, panel_left, panel_right, inverse_factors, active):
    width = inverse_factors.shape[1]
    factor_left = triangle(panel_left, inverse_factors)
    factor_right = triangle(panel_right, inverse_factors)
    change = jnp.zeros(trailing.shape, jnp.float32)
    for panel in range(inverse_factors.shape[0]):
        cols = slice(panel * width, (panel + 1) * width)
        right_part = lax.all_gather(factor_right[:, cols], "row", axis=0, tiled=True)
        left_part = lax.all_gather(factor_left[:, cols], "col", axis=0, tiled=True)
        change = change + dot_nt(left_part, right_part)
    tile_rows, tile_cols = active.shape
    shaped = trailing.astype(jnp.float32).reshape(tile_rows, width, tile_cols, width)
    fresh = shaped - change.reshape(tile_rows, width, tile_cols, width)
    keep = active[:, None, :, None] == 1
    result = jnp.where(keep, fresh, shaped).astype(jnp.bfloat16)
    return result.reshape(trailing.shape)


def flip(chip, mask):
    bit = 1
    while bit <= mask:
        if mask & bit:
            chip = chip + (1 - 2 * ((chip // bit) % 2)) * bit
        bit *= 2
    return chip


def kernel(
    nr, nc, tile_cols,
    tr_hbm, left_hbm, right_hbm, inv_hbm, act_ref, out_ref,
    trv, lv, rv, invv, ih, il, rbuf, lbuf, fbuf, acc, outv,
    in_sem, inv_sem, tr_sem, out_sem, rsend, rrecv, lsend, lrecv, fsend,
):
    panels, width = ih.shape[0], ih.shape[1]
    half = width // 2
    chunks = 2 * panels
    ml, mr = lv.shape[0], rv.shape[0]
    rows = trv.shape[1]
    chips = nc // 2
    z = lax.axis_index("row")
    c = lax.axis_index("col")
    chip, core = c // 2, c % 2
    sib = chip * 2 + 1 - core

    def peer(j):
        return flip(chip, j) * 2 + core

    def other(j):
        return flip(chip, j) * 2 + 1 - core

    def cols(piece):
        return pl.ds(pl.multiple_of(piece * mr, mr), mr)

    barrier = pltpu.get_barrier_semaphore()

    def greet(dev):
        pl.semaphore_signal(barrier, inc=1, device_id=dev, device_id_type=MESH)

    @pl.when(z > 0)
    def _():
        greet((z - 1, c))

    @pl.when(z < nr - 1)
    def _():
        greet((z + 1, c))

    greet((z, sib))
    for j in range(1, chips):
        greet((z, peer(j)))

    load_left = pltpu.make_async_copy(left_hbm, lv, in_sem.at[0])
    load_right = pltpu.make_async_copy(right_hbm, rv, in_sem.at[1])
    load_inv = [
        pltpu.make_async_copy(inv_hbm.at[p], invv.at[p], inv_sem.at[p])
        for p in range(panels)
    ]
    load_left.start()
    load_right.start()
    for cp in load_inv:
        cp.start()
    load_tr = [
        pltpu.make_async_copy(
            tr_hbm.at[:, i * mr : (i + 1) * mr], trv.at[i], tr_sem.at[i]
        )
        for i in range(nr)
    ]
    for cp in load_tr:
        cp.start()

    ends = jnp.where(z > 0, 1, 0) + jnp.where(z < nr - 1, 1, 0)
    pl.semaphore_wait(barrier, ends + chips)

    def right_copy(d, t, q):
        to = z - 1 if d == 0 else z + 1
        origin = z + t if d == 0 else z - t
        src = (
            right_hbm.at[:, q * half : (q + 1) * half]
            if t == 0
            else rbuf.at[origin, q]
        )
        return pltpu.make_async_remote_copy(
            src_ref=src,
            dst_ref=rbuf.at[origin, q],
            send_sem=rsend.at[d, t, q],
            recv_sem=rrecv.at[d, t, q],
            device_id=(to, c),
            device_id_type=MESH,
        )

    def right_sends(d, t):
        if d == 0:
            return jnp.logical_and(z > 0, z + t < nr)
        return jnp.logical_and(z < nr - 1, z - t >= 0)

    def right_has(d, s):
        return z + s < nr if d == 0 else z - s >= 0

    for d in range(2):
        @pl.when(right_sends(d, 0))
        def _():
            for q in range(chunks):
                right_copy(d, 0, q).start()

    def left_copy(p, dev, origin, sems, j):
        return pltpu.make_async_remote_copy(
            src_ref=lbuf.at[p, origin],
            dst_ref=lbuf.at[p, origin],
            send_sem=sems.at[p, j],
            recv_sem=lrecv.at[p, origin],
            device_id=(z, dev),
            device_id_type=MESH,
        )

    def factor(part0, part1, p):
        first = dot_nt(part0, ih[p, :half, :half]) + dot_nt(part0, il[p, :half, :half])
        second = (
            dot_nt(part0, ih[p, half:, :half])
            + dot_nt(part1, ih[p, half:, half:])
            + dot_nt(part0, il[p, half:, :half])
            + dot_nt(part1, il[p, half:, half:])
        )
        return first.astype(jnp.bfloat16), second.astype(jnp.bfloat16)

    load_left.wait()
    for p in range(panels):
        load_inv[p].wait()
        whole = invv[p]
        high = whole.astype(jnp.bfloat16)
        ih[p] = high
        il[p] = (whole - high.astype(jnp.float32)).astype(jnp.bfloat16)
        a = lv[:, p * width : p * width + half]
        b = lv[:, p * width + half : (p + 1) * width]
        first, second = factor(a, b, p)
        lbuf[p, c, :, :half] = first
        lbuf[p, c, :, half:] = second
        for j in range(1, chips):
            left_copy(p, peer(j), c, lsend, j).start()
        left_copy(p, sib, c, lsend, 0).start()

    load_right.wait()
    for p in range(panels):
        a = rv[:, p * width : p * width + half]
        b = rv[:, p * width + half : (p + 1) * width]
        first, second = factor(a, b, p)
        fbuf[p, z, :, :half] = first
        fbuf[p, z, :, half:] = second

    def right_arrive(s, p):
        for d in range(2):
            origin = z + s if d == 0 else z - s

            @pl.when(right_has(d, s))
            def _():
                for h in range(2):
                    q = 2 * p + h
                    right_copy(d, s - 1, q).wait_recv()
                    if s < nr - 1:
                        @pl.when(right_sends(d, s))
                        def _():
                            right_copy(d, s, q).start()
                first, second = factor(rbuf[origin, 2 * p], rbuf[origin, 2 * p + 1], p)
                fbuf[p, origin, :, :half] = first
                fbuf[p, origin, :, half:] = second

    def left_arrive(p):
        for j in range(1, chips):
            left_copy(p, peer(j), peer(j), lsend, j).wait_recv()
            left_copy(p, sib, peer(j), fsend, j).start()

    def left_rest(p):
        for j in range(chips):
            left_copy(p, sib, other(j), lsend, 0).wait_recv()

    def product(p, piece):
        left = lbuf[p].reshape(nc * ml, width)
        return dot_nt(left, fbuf[p, piece])

    def begin(p, piece):
        if p == 0:
            acc[piece] = product(p, piece)
        else:
            acc[piece] += product(p, piece)

    def finish(piece):
        change = product(panels - 1, piece)
        if panels > 1:
            change = acc[piece] + change
        tc = (piece * mr) // width
        for t in range(rows // width):
            span = slice(t * width, (t + 1) * width)
            old = trv[piece, span].astype(jnp.float32)
            keep = jnp.full(old.shape, act_ref[t * tile_cols + tc], jnp.int32) == 1
            new = jnp.where(keep, old - change[span], old)
            outv[piece, span] = new.astype(jnp.bfloat16)
        pltpu.make_async_copy(
            outv.at[piece], out_ref.at[:, cols(piece)], out_sem.at[piece]
        ).start()

    def at_step(s, fn):
        if s == 0:
            fn(z)
            return
        for d in range(2):
            @pl.when(right_has(d, s))
            def _():
                fn(z + s if d == 0 else z - s)

    last = nr - 1
    for s in range(1, last):
        for p in range(panels):
            right_arrive(s, p)
        if s == 1:
            for p in range(panels - 1):
                left_arrive(p)
    if last < 2:
        for p in range(panels - 1):
            left_arrive(p)
    for p in range(panels - 1):
        left_rest(p)
        for s in range(last):
            at_step(s, functools.partial(begin, p))
    left_arrive(panels - 1)
    for cp in load_tr:
        cp.wait()
    for p in range(panels - 1):
        if last > 0:
            right_arrive(last, p)
            at_step(last, functools.partial(begin, p))
    left_rest(panels - 1)
    for s in range(last):
        at_step(s, finish)
    if last > 0:
        right_arrive(last, panels - 1)
        at_step(last, finish)

    for d in range(2):
        for t in range(nr - 1):
            @pl.when(right_sends(d, t))
            def _():
                for q in range(chunks):
                    right_copy(d, t, q).wait_send()
    for p in range(panels):
        for j in range(1, chips):
            left_copy(p, peer(j), c, lsend, j).wait_send()
            left_copy(p, sib, peer(j), fsend, j).wait_send()
        left_copy(p, sib, c, lsend, 0).wait_send()
    for piece in range(nr):
        pltpu.make_async_copy(
            outv.at[piece], out_ref.at[:, piece * mr : (piece + 1) * mr], out_sem.at[piece]
        ).wait()


def local(nr, nc, trailing, panel_left, panel_right, inverse_factors, active):
    panels, width = inverse_factors.shape[:2]
    half = width // 2
    rows, _ = trailing.shape
    ml, depth = panel_left.shape
    mr = panel_right.shape[0]
    chips = nc // 2
    if ml % 16 or mr % 128 or half % 128 or width % mr or nc % 2 or chips & (chips - 1) or nr < 2:
        return local_plain(trailing, panel_left, panel_right, inverse_factors, active)
    bf16, f32 = jnp.bfloat16, jnp.float32
    anywhere = pl.BlockSpec(memory_space=pl.ANY)
    return pl.pallas_call(
        functools.partial(kernel, nr, nc, active.shape[1]),
        out_shape=jax.ShapeDtypeStruct(trailing.shape, bf16),
        in_specs=[anywhere] * 4 + [pl.BlockSpec(memory_space=pltpu.SMEM)],
        out_specs=anywhere,
        scratch_shapes=[
            pltpu.VMEM((nr, rows, mr), bf16),
            pltpu.VMEM((ml, depth), bf16),
            pltpu.VMEM((mr, depth), bf16),
            pltpu.VMEM((panels, width, width), f32),
            pltpu.VMEM((panels, width, width), bf16),
            pltpu.VMEM((panels, width, width), bf16),
            pltpu.VMEM((nr, 2 * panels, mr, half), bf16),
            pltpu.VMEM((panels, nc, ml, width), bf16),
            pltpu.VMEM((panels, nr, mr, width), bf16),
            pltpu.VMEM((nr, rows, mr), f32),
            pltpu.VMEM((nr, rows, mr), bf16),
            pltpu.SemaphoreType.DMA((2,)),
            pltpu.SemaphoreType.DMA((panels,)),
            pltpu.SemaphoreType.DMA((nr,)),
            pltpu.SemaphoreType.DMA((nr,)),
            pltpu.SemaphoreType.DMA((2, nr - 1, 2 * panels)),
            pltpu.SemaphoreType.DMA((2, nr - 1, 2 * panels)),
            pltpu.SemaphoreType.DMA((panels, chips)),
            pltpu.SemaphoreType.DMA((panels, nc)),
            pltpu.SemaphoreType.DMA((panels, chips)),
        ],
        compiler_params=pltpu.CompilerParams(
            collective_id=0, has_side_effects=True, vmem_limit_bytes=40 * 2**20
        ),
        name="trailing_update",
    )(trailing, panel_left, panel_right, inverse_factors, active.reshape(-1))


def solution(mesh):
    in_specs = (
        P("row", "col"),
        P(("row", "col"), None),
        P(("col", "row"), None),
        P(),
        P("row", "col"),
    )
    body = functools.partial(local, mesh.shape["row"], mesh.shape["col"])
    return jax.shard_map(
        body, mesh=mesh, in_specs=in_specs, out_specs=P("row", "col"), check_vma=False
    )
```

time: 71.5 us -> 32.6 us (0.46)
  blocking collectives: 33.5 us -> 0 us
  Pallas kernels: 0 us -> 26 us
  between operations: 13.4 us -> 0.01 us
  matrix products: 12.2 us -> 0 us
  waiting for transfers between devices: 12 us -> 0 us
  local copies, waits for them, and re-layouts: 0.11 us -> 6.34 us
    all_gather x2 -> x0, blocking collectives: 33.5 us -> none  [local(): lax.all_gather(factor_right[:, panel * width:(panel + 1) * width], 'row',...]
    pallas_call x0 -> x1, Pallas kernels: none -> 26 us  [local(): pl.pallas_call(functools.partial(kernel, nr, nc, active.shape[1]), out_sh...]
    dot_general x6 -> x0, matrix products: 12.2 us -> none  [the longest x4 6.86 us: triangle(): jnp.dot(block, inverse_factors[panel].T, precision=lax.Precision.HIGHEST,...]
    all_gather x2 -> x0, waiting for transfers between devices: 12 us -> none  [local(): lax.all_gather(factor_left[:, panel * width:(panel + 1) * width], 'col',...]
    unnamed x6 -> x11, local copies, waits for them, and re-layouts: 0.01 us -> 6.34 us
  transfers between devices with their start and end apart: 2 -> 0, of which waited for: 1 -> 0; matrix products, arithmetic and copies ran while one was open for 9% -> 0% of each run, Pallas kernels for 0% -> 0%
where the time goes in v1:
time: 32.6 us; the launch traced here: 32.3 us
  Pallas kernels  26 us (80%)
  local copies, waits for them, and re-layouts  6.34 us (19%)
    pallas_call x1, Pallas kernels, local(): pl.pallas_call(functools.partial(kernel, nr, nc, active.shape[1]), out_sh...  26 us
    unnamed x11, local copies, waits for them, and re-layouts  6.34 us

profile of v1, /device:TPU:0, one launch (start us, length us, event | category | flops | bytes accessed | tf_op | source)
XLA Modules:
  0.0 32.3 jit_solution(5994864607024066603)
XLA Ops:
  0.0 0.0 copy-start
  0.0 1.6 %copy-done = f32[2,512,512]{2,1,0:T(8,128)S(1)} copy-done((f32[2,512,512]{2,1,0:T(8,128)S(1)}, f32[2,512,512]{2,1,0:T(8,128)}, u32[]{:S(2)}) %copy-start) | copy-done | bytes 2097176
  1.6 0.0 copy-start.1
  1.6 1.2 %copy-done.1 = bf16[1024,512]{1,0:T(8,128)(2,1)S(1)} copy-done((bf16[1024,512]{1,0:T(8,128)(2,1)S(1)}, bf16[1024,512]{1,0:T(8,128)(2,1)}, u32[]{:S(2)}) %copy-start.1) | copy-done | bytes 1048600
  2.8 0.0 copy-start.2
  2.8 0.9 %copy-done.2 = bf16[128,1024]{1,0:T(8,128)(2,1)S(1)} copy-done((bf16[128,1024]{1,0:T(8,128)(2,1)S(1)}, bf16[128,1024]{1,0:T(8,128)(2,1)}, u32[]{:S(2)}) %copy-start.2) | copy-done | bytes 262168
  3.8 0.0 copy-start.3
  3.8 0.9 %copy-done.3 = bf16[128,1024]{1,0:T(8,128)(2,1)S(1)} copy-done((bf16[128,1024]{1,0:T(8,128)(2,1)S(1)}, bf16[128,1024]{1,0:T(8,128)(2,1)}, u32[]{:S(2)}) %copy-start.3) | copy-done | bytes 262168
  4.7 0.0 copy-start.4
  4.7 0.7 %copy-done.4 = s32[2,1]{0,1:T(1,128)S(1)} copy-done((s32[2,1]{0,1:T(1,128)S(1)}, s32[2,1]{0,1:T(1,128)}, u32[]{:S(2)}) %copy-start.4) | copy-done | bytes 32
  5.4 26.0 %trailing_update.1 = bf16[1024,512]{1,0:T(8,128)(2,1)S(1)} custom-call(bf16[1024,512]{1,0:T(8,128)(2,1)S(1)} %copy-done.1, bf16[128,1024]{1,0:T(8,128)(2,1)S(1)} %copy-done.2, bf16[128,1024]{1,0:T(8,128)(2,1)S(1)} %copy-done.3, f32[2,512,512]{2,1,0:T(8,128)S(1)} %copy-done, s32[2]{0:T(128)S(1)} %bitcast.1), custom_call_target="tpu_custom_call" | custom-call | tf_op jit(solution)/shard_map/trailing_update/pallas_call | solution.py:317
  31.3 1.0 %copy.7 = bf16[1024,512]{1,0:T(8,128)(2,1)} copy(bf16[1024,512]{1,0:T(8,128)(2,1)S(1)} %trailing_update.1) | data formatting | bytes 2097152
Async XLA Ops:
  0.0 1.6 %copy-start = (f32[2,512,512]{2,1,0:T(8,128)S(1)}, f32[2,512,512]{2,1,0:T(8,128)}, u32[]{:S(2)}) copy-start(f32[2,512,512]{2,1,0:T(8,128)} %inv_hbm.1) | copy-start | bytes 6291460
  1.6 1.2 %copy-start.1 = (bf16[1024,512]{1,0:T(8,128)(2,1)S(1)}, bf16[1024,512]{1,0:T(8,128)(2,1)}, u32[]{:S(2)}) copy-start(bf16[1024,512]{1,0:T(8,128)(2,1)} %tr_hbm.1) | copy-start | bytes 3145732
  2.8 0.9 %copy-start.2 = (bf16[128,1024]{1,0:T(8,128)(2,1)S(1)}, bf16[128,1024]{1,0:T(8,128)(2,1)}, u32[]{:S(2)}) copy-start(bf16[128,1024]{1,0:T(8,128)(2,1)} %left_hbm.1) | copy-start | bytes 786436
  3.8 0.9 %copy-start.3 = (bf16[128,1024]{1,0:T(8,128)(2,1)S(1)}, bf16[128,1024]{1,0:T(8,128)(2,1)}, u32[]{:S(2)}) copy-start(bf16[128,1024]{1,0:T(8,128)(2,1)} %right_hbm.1) | copy-start | bytes 786436
  4.7 0.7 %copy-start.4 = (s32[2,1]{0,1:T(1,128)S(1)}, s32[2,1]{0,1:T(1,128)}, u32[]{:S(2)}) copy-start(s32[2,1]{0,1:T(1,128)} %param.9) | copy-start | bytes 28

commit v2 on v1

--- a/solution.py
+++ b/solution.py
@@ -107,10 +107,11 @@
         pltpu.make_async_copy(inv_hbm.at[p], invv.at[p], inv_sem.at[p])
         for p in range(panels)
     ]
+    load_right.start()
+    for cp in load_inv[1:]:
+        cp.start()
     load_left.start()
-    load_right.start()
-    for cp in load_inv:
-        cp.start()
+    load_inv[0].start()
     load_tr = [
         pltpu.make_async_copy(
             tr_hbm.at[:, i * mr : (i + 1) * mr], trv.at[i], tr_sem.at[i]
@@ -126,14 +127,11 @@
     def right_copy(d, t, q):
         to = z - 1 if d == 0 else z + 1
         origin = z + t if d == 0 else z - t
-        src = (
-            right_hbm.at[:, q * half : (q + 1) * half]
-            if t == 0
-            else rbuf.at[origin, q]
-        )
+        slot = rbuf.at[origin, q] if q < 2 else fbuf.at[q, origin]
+        own = q < 2 and t == 0
         return pltpu.make_async_remote_copy(
-            src_ref=src,
-            dst_ref=rbuf.at[origin, q],
+            src_ref=right_hbm.at[:, q * half : (q + 1) * half] if own else slot,
+            dst_ref=slot,
             send_sem=rsend.at[d, t, q],
             recv_sem=rrecv.at[d, t, q],
             device_id=(to, c),
@@ -148,11 +146,14 @@
     def right_has(d, s):
         return z + s < nr if d == 0 else z - s >= 0
 
-    for d in range(2):
-        @pl.when(right_sends(d, 0))
-        def _():
-            for q in range(chunks):
-                right_copy(d, 0, q).start()
+    def right_own(qs):
+        for d in range(2):
+            @pl.when(right_sends(d, 0))
+            def _():
+                for q in qs:
+                    right_copy(d, 0, q).start()
+
+    right_own(range(2))
 
     def left_copy(p, dev, origin, sems, j):
         return pltpu.make_async_remote_copy(
@@ -174,46 +175,61 @@
         )
         return first.astype(jnp.bfloat16), second.astype(jnp.bfloat16)
 
-    load_left.wait()
-    for p in range(panels):
+    def halves(ref, p):
+        return (
+            ref[:, p * width : p * width + half],
+            ref[:, p * width + half : (p + 1) * width],
+        )
+
+    def factor_right(a, b, p, piece):
+        fbuf[2 * p, piece], fbuf[2 * p + 1, piece] = factor(a, b, p)
+
+    def split(p):
         load_inv[p].wait()
         whole = invv[p]
         high = whole.astype(jnp.bfloat16)
         ih[p] = high
         il[p] = (whole - high.astype(jnp.float32)).astype(jnp.bfloat16)
-        a = lv[:, p * width : p * width + half]
-        b = lv[:, p * width + half : (p + 1) * width]
-        first, second = factor(a, b, p)
+
+    load_right.wait()
+    for p in range(1, panels):
+        split(p)
+        factor_right(*halves(rv, p), p, z)
+        right_own((2 * p, 2 * p + 1))
+
+    load_left.wait()
+    for p in range(panels):
+        if p == 0:
+            split(p)
+        first, second = factor(*halves(lv, p), p)
         lbuf[p, c, :, :half] = first
         lbuf[p, c, :, half:] = second
         for j in range(1, chips):
             left_copy(p, peer(j), c, lsend, j).start()
         left_copy(p, sib, c, lsend, 0).start()
-
-    load_right.wait()
-    for p in range(panels):
-        a = rv[:, p * width : p * width + half]
-        b = rv[:, p * width + half : (p + 1) * width]
-        first, second = factor(a, b, p)
-        fbuf[p, z, :, :half] = first
-        fbuf[p, z, :, half:] = second
-
-    def right_arrive(s, p):
+    factor_right(*halves(rv, 0), 0, z)
+
+    def at_step(s, fn):
+        if s == 0:
+            fn(0, z)
+            return
         for d in range(2):
-            origin = z + s if d == 0 else z - s
-
             @pl.when(right_has(d, s))
             def _():
-                for h in range(2):
-                    q = 2 * p + h
-                    right_copy(d, s - 1, q).wait_recv()
-                    if s < nr - 1:
-                        @pl.when(right_sends(d, s))
-                        def _():
-                            right_copy(d, s, q).start()
-                first, second = factor(rbuf[origin, 2 * p], rbuf[origin, 2 * p + 1], p)
-                fbuf[p, origin, :, :half] = first
-                fbuf[p, origin, :, half:] = second
+                fn(d, z + s if d == 0 else z - s)
+
+    def right_arrive(s, qs):
+        def take(d, origin):
+            for q in qs:
+                right_copy(d, s - 1, q).wait_recv()
+                if s < nr - 1:
+                    @pl.when(right_sends(d, s))
+                    def _():
+                        right_copy(d, s, q).start()
+            if 0 in qs:
+                factor_right(rbuf[origin, 0], rbuf[origin, 1], 0, origin)
+
+        at_step(s, take)
 
     def left_arrive(p):
         for j in range(1, chips):
@@ -224,19 +240,29 @@
         for j in range(chips):
             left_copy(p, sib, other(j), lsend, 0).wait_recv()
 
-    def product(p, piece):
-        left = lbuf[p].reshape(nc * ml, width)
-        return dot_nt(left, fbuf[p, piece])
-
-    def begin(p, piece):
-        if p == 0:
-            acc[piece] = product(p, piece)
+    def product(qs, piece):
+        total = None
+        for q in qs:
+            lo = (q % 2) * half
+            left = lbuf[q // 2, :, :, lo : lo + half].reshape(nc * ml, half)
+            part = dot_nt(left, fbuf[q, piece])
+            total = part if total is None else total + part
+        return total
+
+    def store(piece):
+        return pltpu.make_async_copy(
+            outv.at[piece], out_ref.at[:, cols(piece)], out_sem.at[piece]
+        )
+
+    def begin(qs, d, piece):
+        if 0 in qs:
+            acc[piece] = product(qs, piece)
         else:
-            acc[piece] += product(p, piece)
-
-    def finish(piece):
-        change = product(panels - 1, piece)
-        if panels > 1:
+            acc[piece] += product(qs, piece)
+
+    def finish(qs, d, piece):
+        change = product(qs, piece)
+        if 0 not in qs:
             change = acc[piece] + change
         tc = (piece * mr) // width
         for t in range(rows // width):
@@ -245,23 +271,17 @@
             keep = jnp.full(old.shape, act_ref[t * tile_cols + tc], jnp.int32) == 1
             new = jnp.where(keep, old - change[span], old)
             outv[piece, span] = new.astype(jnp.bfloat16)
-        pltpu.make_async_copy(
-            outv.at[piece], out_ref.at[:, cols(piece)], out_sem.at[piece]
-        ).start()
-
-    def at_step(s, fn):
-        if s == 0:
-            fn(z)
-            return
-        for d in range(2):
-            @pl.when(right_has(d, s))
-            def _():
-                fn(z + s if d == 0 else z - s)
+        store(piece).start()
+
+    def panel(p):
+        return (2 * p, 2 * p + 1)
+
+    def add(fn, s, qs):
+        at_step(s, functools.partial(fn, qs))
 
     last = nr - 1
     for s in range(1, last):
-        for p in range(panels):
-            right_arrive(s, p)
+        right_arrive(s, range(chunks))
         if s == 1:
             for p in range(panels - 1):
                 left_arrive(p)
@@ -271,20 +291,24 @@
     for p in range(panels - 1):
         left_rest(p)
         for s in range(last):
-            at_step(s, functools.partial(begin, p))
+            add(begin, s, panel(p))
     left_arrive(panels - 1)
     for cp in load_tr:
         cp.wait()
     for p in range(panels - 1):
-        if last > 0:
-            right_arrive(last, p)
-            at_step(last, functools.partial(begin, p))
+        right_arrive(last, panel(p))
+        add(begin, last, panel(p))
     left_rest(panels - 1)
     for s in range(last):
-        at_step(s, finish)
-    if last > 0:
-        right_arrive(last, panels - 1)
-        at_step(last, finish)
+        add(finish, s, panel(panels - 1))
+    if panels > 1:
+        right_arrive(last, (chunks - 2,))
+        add(begin, last, (chunks - 2,))
+        right_arrive(last, (chunks - 1,))
+        add(finish, last, (chunks - 1,))
+    else:
+        right_arrive(last, panel(0))
+        add(finish, last, panel(0))
 
     for d in range(2):
         for t in range(nr - 1):
@@ -297,10 +321,8 @@
             left_copy(p, peer(j), c, lsend, j).wait_send()
             left_copy(p, sib, peer(j), fsend, j).wait_send()
         left_copy(p, sib, c, lsend, 0).wait_send()
-    for piece in range(nr):
-        pltpu.make_async_copy(
-            outv.at[piece], out_ref.at[:, piece * mr : (piece + 1) * mr], out_sem.at[piece]
-        ).wait()
+    for s in range(nr):
+        at_step(s, lambda d, piece: store(piece).wait())
 
 
 def local(nr, nc, trailing, panel_left, panel_right, inverse_factors, active):
@@ -326,9 +348,9 @@
             pltpu.VMEM((panels, width, width), f32),
             pltpu.VMEM((panels, width, width), bf16),
             pltpu.VMEM((panels, width, width), bf16),
-            pltpu.VMEM((nr, 2 * panels, mr, half), bf16),
+            pltpu.VMEM((nr, 2, mr, half), bf16),
             pltpu.VMEM((panels, nc, ml, width), bf16),
-            pltpu.VMEM((panels, nr, mr, width), bf16),
+            pltpu.VMEM((2 * panels, nr, mr, half), bf16),
             pltpu.VMEM((nr, rows, mr), f32),
             pltpu.VMEM((nr, rows, mr), bf16),
             pltpu.SemaphoreType.DMA((2,)),
@@ -342,7 +364,7 @@
             pltpu.SemaphoreType.DMA((panels, chips)),
         ],
         compiler_params=pltpu.CompilerParams(
-            collective_id=0, has_side_effects=True, vmem_limit_bytes=40 * 2**20
+            collective_id=0, has_side_effects=True, vmem_limit_bytes=58 * 2**20
         ),
         name="trailing_update",
     )(trailing, panel_left, panel_right, inverse_factors, active.reshape(-1))

time: 32.6 us -> 28.7 us (0.88)
  local copies, waits for them, and re-layouts: 6.34 us -> 2.26 us
    unnamed x11 -> x1, local copies, waits for them, and re-layouts: 6.34 us -> 2.26 us
where the time goes in v2:
time: 28.7 us; the launch traced here: 28.6 us
  Pallas kernels  26.3 us (92%)
  local copies, waits for them, and re-layouts  2.26 us (8%)
    pallas_call x1, Pallas kernels, local(): pl.pallas_call(functools.partial(kernel, nr, nc, active.shape[1]), out_sh...  26.3 us
    unnamed x1, local copies, waits for them, and re-layouts  2.26 us

profile of v2, /device:TPU:0, one launch (start us, length us, event | category | flops | bytes accessed | tf_op | source)
XLA Modules:
  0.0 28.6 jit_solution(3566362842192991837)
XLA Ops:
  0.0 26.3 %trailing_update.1 = bf16[1024,512]{1,0:T(8,128)(2,1)} custom-call(bf16[1024,512]{1,0:T(8,128)(2,1)} %tr_hbm.1, bf16[128,1024]{1,0:T(8,128)(2,1)} %left_hbm.1, bf16[128,1024]{1,0:T(8,128)(2,1)} %right_hbm.1, f32[2,512,512]{2,1,0:T(8,128)} %inv_hbm.1, s32[2]{0:T(128)} %bitcast.1), custom_call_target="tpu_custom_call" | custom-call | tf_op jit(solution)/shard_map/trailing_update/pallas_call | solution.py:339
  26.3 2.3 %copy.7 = bf16[1024,512]{1,0:T(8,128)(2,1)} copy(bf16[1024,512]{1,0:T(8,128)(2,1)} %trailing_update.1) | data formatting | bytes 2097152
